TPU v7x, 512 devices: a whole 4x8x8 slice. The times are simulated.
512 devices in a mesh: bias: 8 (over z_lo, x), gx: 8 (over z_hi, core), gy: 8 (over y).
Axes of the slice: x: 4, y: 8, z: 8 (z_hi: 4, z_lo: 2; z = z_hi * 2 + z_lo), core: 2. Of those that a mesh axis runs over, the one named last changes fastest.
Arguments:
- source: bfloat16 [8, 16, 24, 32, 256], P('bias', 'gx', 'gy'), may hold values from -6 to 6
- inverse: bfloat16 [8, 16, 24, 256, 256], P('bias', 'gx', 'gy'), may hold values from -0.375 to 0.375
- coupling: bfloat16 [8, 16, 24, 4, 256, 256], P('bias', 'gx', 'gy'), may hold values from -0.1875 to 0.1875
- sensitivity: float32 [8, 16, 24, 256], P('bias', 'gx', 'gy'), may hold values from -6 to 6
Outputs:
- adjoint_out: bfloat16 [8, 16, 24, 32, 256], P('bias', 'gx', 'gy')
- doping_grad: float32 [16, 24, 2048], P('gx', 'gy', 'bias')
All inputs are finite; a program needn't handle non-finite values.
Results may differ from a plain program's by a relative error of at most 0.02.
Values may be sent and summed in bfloat16 or wider, within the bound.
A program may use at most 64 MiB of HBM per device.

v0:
```python
import jax
import jax.numpy as jnp
from jax import lax
from jax.sharding import PartitionSpec as P

VARS = 4
ITERS = 3


def shifted(block, axis, distance):
    devices = range(lax.axis_size(axis))
    route = [(i - distance, i) for i in devices if i - distance in devices]
    return lax.ppermute(block, axis, route)


def shards(source, inverse, coupling, sensitivity):
    source_b = source[0]
    inverse_b = inverse[0]
    coupling_b = coupling[0]
    source_f = source_b.astype(jnp.float32)
    adjoint = jnp.einsum(
        "xyru,xyuv->xyrv", source_b, inverse_b, preferred_element_type=jnp.float32
    ).astype(jnp.bfloat16)
    for step in range(ITERS):
        products = jnp.einsum(
            "xyru,xyduv->xydrv", adjoint, coupling_b, preferred_element_type=jnp.float32
        ).astype(jnp.bfloat16)
        west_part = shifted(products[-1:, :, 0], "gx", 1)
        east_part = shifted(products[:1, :, 1], "gx", -1)
        south_part = shifted(products[:, -1:, 2], "gy", 1)
        north_part = shifted(products[:, :1, 3], "gy", -1)
        plus_x = jnp.concatenate([west_part, products[:-1, :, 0]], axis=0)
        minus_x = jnp.concatenate([products[1:, :, 1], east_part], axis=0)
        plus_y = jnp.concatenate([south_part, products[:, :-1, 2]], axis=1)
        minus_y = jnp.concatenate([products[:, 1:, 3], north_part], axis=1)
        incoming = (
            plus_x.astype(jnp.float32)
            + minus_x.astype(jnp.float32)
            + plus_y.astype(jnp.float32)
            + minus_y.astype(jnp.float32)
        )
        update = (source_f - incoming).astype(jnp.bfloat16)
        adjoint = jnp.einsum(
            "xyru,xyuv->xyrv", update, inverse_b, preferred_element_type=jnp.float32
        ).astype(jnp.bfloat16)
    blocks_x = adjoint.shape[0]
    blocks_y = adjoint.shape[1]
    sides = adjoint.shape[2]
    width = adjoint.shape[3] // VARS
    shaped = adjoint.astype(jnp.float32).reshape(blocks_x, blocks_y, sides, VARS, width)
    weights = sensitivity[0].reshape(blocks_x, blocks_y, 1, VARS, width)
    terms = jnp.sum(shaped * weights, axis=3).reshape(blocks_x, blocks_y, sides * width)
    summed = lax.psum(terms.astype(jnp.bfloat16), "bias").astype(jnp.float32)
    share = summed.shape[2] // lax.axis_size("bias")
    doping_grad = lax.dynamic_slice_in_dim(summed, lax.axis_index("bias") * share, share, 2)
    return (adjoint[None], doping_grad)


def solution(mesh):
    placed = (
        P("bias", "gx", "gy", None, None),
        P("bias", "gx", "gy", None, None),
        P("bias", "gx", "gy", None, None, None),
        P("bias", "gx", "gy", None),
    )
    return jax.shard_map(
        shards,
        mesh=mesh,
        in_specs=placed,
        out_specs=(P("bias", "gx", "gy", None, None), P("gx", "gy", "bias")),
        check_vma=False,
    )
```

profile of v0, /device:TPU:272, one launch (start us, length us, event | category | flops | bytes accessed | tf_op | source)
XLA Modules:
  0.0 102.6 jit_solution(6495505845985194345)
XLA Ops:
  0.6 1.9 %copy-done = bf16[1,2,3,4,256,256]{5,4,3,2,1,0:T(8,128)(2,1)S(1)} copy-done((bf16[1,2,3,4,256,256]{5,4,3,2,1,0:T(8,128)(2,1)S(1)}, bf16[1,2,3,4,256,256]{5,4,3,2,1,0:T(8,128)(2,1)}, u32[]{:S(2)}) %copy-start) | copy-done | bytes 3145752
  2.5 2.0 %fusion.10 = bf16[2,3,4,32,256]{4,3,2,1,0:T(8,128)(2,1)S(1)} fusion(bf16[1,2,3,256,256]{4,3,2,1,0:T(8,128)(2,1)} %param.5, bf16[1,2,3,32,256]{4,3,2,1,0:T(8,128)(2,1)} %param.4, bf16[1,2,3,4,256,256]{5,4,3,2,1,0:T(8,128)(2,1)S(1)} %copy-done), kind=kOutput, calls=%fused_computation.7 | convolution fusion | flops 126074880 | bytes 4423680 | tf_op jit(solution)/shard_map/xyru,xyduv->xydrv/dot_general | solution.py:25
  5.2 1.9 %collective-permute-start = (bf16[1,3,32,256]{3,2,1,0:T(8,128)(2,1)}, bf16[1,3,32,256]{3,2,1,0:T(8,128)(2,1)}, u32[]{:S(2)}, u32[]{:S(2)}) collective-permute-start(bf16[1,3,32,256]{3,2,1,0:T(8,128)(2,1)} %get-tuple-element.24), channel_id=1, source_target_pairs={{0,8},{8,16},{16,24},{24,32},{32,40},{40,48},{48,56},{1,9},{9,17},... | collective-permute-start | bytes 147464 | tf_op jit(solution)/shard_map/ppermute | solution.py:13
  7.1 5.8 %collective-permute-start.1 = (bf16[1,3,32,256]{3,2,1,0:T(8,128)(2,1)}, bf16[1,3,32,256]{3,2,1,0:T(8,128)(2,1)}, u32[]{:S(2)}, u32[]{:S(2)}) collective-permute-start(bf16[1,3,32,256]{3,2,1,0:T(8,128)(2,1)} %get-tuple-element.25), channel_id=1, source_target_pairs={{8,0},{16,8},{24,16},{32,24},{40,32},{48,40},{56,48},{9,1},{17,9},... | collective-permute-start | bytes 147464 | tf_op jit(solution)/shard_map/ppermute | solution.py:13
  13.5 2.3 %collective-permute-start.3 = (bf16[2,1,32,256]{3,2,0,1:T(8,128)(2,1)}, bf16[2,1,32,256]{3,2,0,1:T(8,128)(2,1)}, u32[]{:S(2)}, u32[]{:S(2)}) collective-permute-start(bf16[2,1,32,256]{3,2,0,1:T(8,128)(2,1)} %get-tuple-element.20), channel_id=1, source_target_pairs={{1,0},{2,1},{3,2},{4,3},{5,4},{6,5},{7,6},{9,8},{10,9},{11,10},{12... | collective-permute-start | bytes 98312 | tf_op jit(solution)/shard_map/ppermute | solution.py:13
  15.9 3.5 %collective-permute-start.2 = (bf16[2,1,32,256]{3,2,1,0:T(8,128)(2,1)}, bf16[2,1,32,256]{3,2,1,0:T(8,128)(2,1)}, u32[]{:S(2)}, u32[]{:S(2)}) collective-permute-start(bf16[2,1,32,256]{3,2,1,0:T(8,128)(2,1)} %get-tuple-element.21), channel_id=1, source_target_pairs={{0,1},{1,2},{2,3},{3,4},{4,5},{5,6},{6,7},{8,9},{9,10},{10,11},{11... | collective-permute-start | bytes 98312 | tf_op jit(solution)/shard_map/ppermute | solution.py:13
  20.8 1.2 %collective-permute-done.2 = bf16[2,1,32,256]{3,2,1,0:T(8,128)(2,1)} collective-permute-done((bf16[2,1,32,256]{3,2,1,0:T(8,128)(2,1)}, bf16[2,1,32,256]{3,2,1,0:T(8,128)(2,1)}, u32[]{:S(2)}, u32[]{:S(2)}) %collective-permute-start.2) | collective-permute-done | bytes 32800 | tf_op jit(solution)/shard_map/ppermute | solution.py:13
  22.0 1.6 %fusion.18 = bf16[2,3,32,256,1]{3,2,1,0,4:T(8,128)(2,1)S(1)} fusion(bf16[1,2,3,256,256]{4,3,2,1,0:T(8,128)(2,1)} %param.5, bf16[1,3,32,256]{3,2,1,0:T(8,128)(2,1)} %get-tuple-element.23, bf16[1,3,32,256]{3,2,1,0:T(8,128)(2,1)} %collective-permute-done, bf16[1,3,32,256]{3,2,1,0:T(8,128)(2,1)} %collective-permute-done.1, ...), kind=kOutput, calls=%fused_computation.15 | convolution fusion | flops 25903104 | bytes 1376256 | tf_op jit(solution)/shard_map/xyru,xyuv->xyrv/dot_general | solution.py:43
  24.3 2.1 %collective-permute-start.4 = (bf16[1,3,32,256]{3,2,0,1:T(8,128)(2,1)S(1)}, bf16[1,3,32,256]{3,2,0,1:T(8,128)(2,1)S(1)}, u32[]{:S(2)}, u32[]{:S(2)}) collective-permute-start(bf16[1,3,32,256]{3,2,0,1:T(8,128)(2,1)S(1)} %get-tuple-element.16), channel_id=1, source_target_pairs={{0,8},{8,16},{16,24},{24,32},{32,40},{40,48},{48,56},{1,9},{9,17},... | collective-permute-start | bytes 147464 | tf_op jit(solution)/shard_map/ppermute | solution.py:13
  26.4 5.8 %collective-permute-start.5 = (bf16[1,3,32,256]{3,2,0,1:T(8,128)(2,1)S(1)}, bf16[1,3,32,256]{3,2,0,1:T(8,128)(2,1)S(1)}, u32[]{:S(2)}, u32[]{:S(2)}) collective-permute-start(bf16[1,3,32,256]{3,2,0,1:T(8,128)(2,1)S(1)} %get-tuple-element.17), channel_id=1, source_target_pairs={{8,0},{16,8},{24,16},{32,24},{40,32},{48,40},{56,48},{9,1},{17,9},... | collective-permute-start | bytes 147464 | tf_op jit(solution)/shard_map/ppermute | solution.py:13
  32.2 4.0 %collective-permute-start.6 = (bf16[2,1,32,256]{3,2,0,1:T(8,128)(2,1)S(1)}, bf16[2,1,32,256]{3,2,0,1:T(8,128)(2,1)S(1)}, u32[]{:S(2)}, u32[]{:S(2)}) collective-permute-start(bf16[2,1,32,256]{3,2,0,1:T(8,128)(2,1)S(1)} %get-tuple-element.13), channel_id=1, source_target_pairs={{0,1},{1,2},{2,3},{3,4},{4,5},{5,6},{6,7},{8,9},{9,10},{10,11},{11... | collective-permute-start | bytes 98312 | tf_op jit(solution)/shard_map/ppermute | solution.py:13
  36.1 1.9 %collective-permute-start.7 = (bf16[2,1,32,256]{3,2,1,0:T(8,128)(2,1)S(1)}, bf16[2,1,32,256]{3,2,1,0:T(8,128)(2,1)S(1)}, u32[]{:S(2)}, u32[]{:S(2)}) collective-permute-start(bf16[2,1,32,256]{3,2,1,0:T(8,128)(2,1)S(1)} %get-tuple-element.12), channel_id=1, source_target_pairs={{1,0},{2,1},{3,2},{4,3},{5,4},{6,5},{7,6},{9,8},{10,9},{11,10},{12... | collective-permute-start | bytes 98312 | tf_op jit(solution)/shard_map/ppermute | solution.py:13
  38.1 5.4 %collective-permute-done.7 = bf16[2,1,32,256]{3,2,1,0:T(8,128)(2,1)S(1)} collective-permute-done((bf16[2,1,32,256]{3,2,1,0:T(8,128)(2,1)S(1)}, bf16[2,1,32,256]{3,2,1,0:T(8,128)(2,1)S(1)}, u32[]{:S(2)}, u32[]{:S(2)}) %collective-permute-start.7) | collective-permute-done | bytes 32800 | tf_op jit(solution)/shard_map/ppermute | solution.py:13
  43.5 1.1 %fusion.19 = bf16[2,3,32,256,1]{3,2,1,0,4:T(8,128)(2,1)S(1)} fusion(bf16[1,2,3,256,256]{4,3,2,1,0:T(8,128)(2,1)S(1)} %copy-done.1, bf16[2,1,32,256]{3,2,1,0:T(8,128)(2,1)S(1)} %collective-permute-done.7, bf16[1,2,3,32,256]{4,3,2,1,0:T(8,128)(2,1)} %param.4, bf16[1,3,32,256]{3,2,0,1:T(8,128)(2,1)S(1)} %get-tuple-element.15, ...), kind=kOutput, calls=%fused_computation.16 | convolution fusion | flops 26001408 | bytes 1376256 | tf_op jit(solution)/shard_map/xyru,xyuv->xyrv/dot_general | solution.py:43
  45.3 1.9 %collective-permute-start.8 = (bf16[1,3,32,256]{3,2,0,1:T(8,128)(2,1)S(1)}, bf16[1,3,32,256]{3,2,0,1:T(8,128)(2,1)S(1)}, u32[]{:S(2)}, u32[]{:S(2)}) collective-permute-start(bf16[1,3,32,256]{3,2,0,1:T(8,128)(2,1)S(1)} %get-tuple-element.8), channel_id=1, source_target_pairs={{0,8},{8,16},{16,24},{24,32},{32,40},{40,48},{48,56},{1,9},{9,17},... | collective-permute-start | bytes 147464 | tf_op jit(solution)/shard_map/ppermute | solution.py:13
  47.2 5.8 %collective-permute-start.9 = (bf16[1,3,32,256]{3,2,0,1:T(8,128)(2,1)S(1)}, bf16[1,3,32,256]{3,2,0,1:T(8,128)(2,1)S(1)}, u32[]{:S(2)}, u32[]{:S(2)}) collective-permute-start(bf16[1,3,32,256]{3,2,0,1:T(8,128)(2,1)S(1)} %get-tuple-element.9), channel_id=1, source_target_pairs={{8,0},{16,8},{24,16},{32,24},{40,32},{48,40},{56,48},{9,1},{17,9},... | collective-permute-start | bytes 147464 | tf_op jit(solution)/shard_map/ppermute | solution.py:13
  53.0 5.1 %collective-permute-start.10 = (bf16[2,1,32,256]{3,2,0,1:T(8,128)(2,1)S(1)}, bf16[2,1,32,256]{3,2,0,1:T(8,128)(2,1)S(1)}, u32[]{:S(2)}, u32[]{:S(2)}) collective-permute-start(bf16[2,1,32,256]{3,2,0,1:T(8,128)(2,1)S(1)} %get-tuple-element.5), channel_id=1, source_target_pairs={{0,1},{1,2},{2,3},{3,4},{4,5},{5,6},{6,7},{8,9},{9,10},{10,11},{11... | collective-permute-start | bytes 98312 | tf_op jit(solution)/shard_map/ppermute | solution.py:13
  58.1 1.9 %collective-permute-start.11 = (bf16[2,1,32,256]{3,2,1,0:T(8,128)(2,1)S(1)}, bf16[2,1,32,256]{3,2,1,0:T(8,128)(2,1)S(1)}, u32[]{:S(2)}, u32[]{:S(2)}) collective-permute-start(bf16[2,1,32,256]{3,2,1,0:T(8,128)(2,1)S(1)} %get-tuple-element.4), channel_id=1, source_target_pairs={{1,0},{2,1},{3,2},{4,3},{5,4},{6,5},{7,6},{9,8},{10,9},{11,10},{12... | collective-permute-start | bytes 98312 | tf_op jit(solution)/shard_map/ppermute | solution.py:13
  60.1 3.9 %collective-permute-done.11 = bf16[2,1,32,256]{3,2,1,0:T(8,128)(2,1)S(1)} collective-permute-done((bf16[2,1,32,256]{3,2,1,0:T(8,128)(2,1)S(1)}, bf16[2,1,32,256]{3,2,1,0:T(8,128)(2,1)S(1)}, u32[]{:S(2)}, u32[]{:S(2)}) %collective-permute-start.11) | collective-permute-done | bytes 32800 | tf_op jit(solution)/shard_map/ppermute | solution.py:13
  64.0 0.9 convolution_convert_fusion.1
  64.9 1.1 %reshape.16 = f32[2,3,32,4,64]{4,3,2,1,0:T(4,128)S(1)} reshape(bf16[2,3,32,256]{3,2,1,0:T(8,128)(2,1)} %convolution_convert_fusion.1) | data formatting | bytes 294912 | tf_op jit(solution)/shard_map/reshape | solution.py:50
  66.0 0.9 multiply_reduce_fusion
  66.9 0.9 reshape.20
  67.8 34.2 %psum.7 = bf16[2,3,2048]{2,0,1:T(2,128)(2,1)S(1)} all-reduce(bf16[2,3,2048]{2,0,1:T(2,128)(2,1)S(1)} %copy.80), channel_id=1, replica_groups=mesh['bias'=8,'gx'=8,'gy'=8] {'bias'}, use_global_device_ids=true, to_apply=%region_1.0 | all-reduce | flops 12288 | bytes 49152 | tf_op jit(solution)/shard_map/psum | solution.py:53
  (28 shorter events, 4.8 us)
Async XLA Ops:
  0.6 1.9 %copy-start = (bf16[1,2,3,4,256,256]{5,4,3,2,1,0:T(8,128)(2,1)S(1)}, bf16[1,2,3,4,256,256]{5,4,3,2,1,0:T(8,128)(2,1)}, u32[]{:S(2)}) copy-start(bf16[1,2,3,4,256,256]{5,4,3,2,1,0:T(8,128)(2,1)} %param.6) | copy-start | bytes 9437188
  5.2 16.8 %collective-permute-start = (bf16[1,3,32,256]{3,2,1,0:T(8,128)(2,1)}, bf16[1,3,32,256]{3,2,1,0:T(8,128)(2,1)}, u32[]{:S(2)}, u32[]{:S(2)}) collective-permute-start(bf16[1,3,32,256]{3,2,1,0:T(8,128)(2,1)} %get-tuple-element.24), channel_id=1, source_target_pairs={{0,8},{8,16},{16,24},{24,32},{32,40},{40,48},{48,56},{1,9},{9,17},... | collective-permute-start | bytes 147464 | tf_op jit(solution)/shard_map/ppermute | solution.py:13
  7.1 14.9 %collective-permute-start.1 = (bf16[1,3,32,256]{3,2,1,0:T(8,128)(2,1)}, bf16[1,3,32,256]{3,2,1,0:T(8,128)(2,1)}, u32[]{:S(2)}, u32[]{:S(2)}) collective-permute-start(bf16[1,3,32,256]{3,2,1,0:T(8,128)(2,1)} %get-tuple-element.25), channel_id=1, source_target_pairs={{8,0},{16,8},{24,16},{32,24},{40,32},{48,40},{56,48},{9,1},{17,9},... | collective-permute-start | bytes 147464 | tf_op jit(solution)/shard_map/ppermute | solution.py:13
  13.5 7.3 %collective-permute-start.3 = (bf16[2,1,32,256]{3,2,0,1:T(8,128)(2,1)}, bf16[2,1,32,256]{3,2,0,1:T(8,128)(2,1)}, u32[]{:S(2)}, u32[]{:S(2)}) collective-permute-start(bf16[2,1,32,256]{3,2,0,1:T(8,128)(2,1)} %get-tuple-element.20), channel_id=1, source_target_pairs={{1,0},{2,1},{3,2},{4,3},{5,4},{6,5},{7,6},{9,8},{10,9},{11,10},{12... | collective-permute-start | bytes 98312 | tf_op jit(solution)/shard_map/ppermute | solution.py:13
  15.9 6.1 %collective-permute-start.2 = (bf16[2,1,32,256]{3,2,1,0:T(8,128)(2,1)}, bf16[2,1,32,256]{3,2,1,0:T(8,128)(2,1)}, u32[]{:S(2)}, u32[]{:S(2)}) collective-permute-start(bf16[2,1,32,256]{3,2,1,0:T(8,128)(2,1)} %get-tuple-element.21), channel_id=1, source_target_pairs={{0,1},{1,2},{2,3},{3,4},{4,5},{5,6},{6,7},{8,9},{9,10},{10,11},{11... | collective-permute-start | bytes 98312 | tf_op jit(solution)/shard_map/ppermute | solution.py:13
  20.8 22.7 %copy-start.1 = (bf16[1,2,3,256,256]{4,3,2,1,0:T(8,128)(2,1)S(1)}, bf16[1,2,3,256,256]{4,3,2,1,0:T(8,128)(2,1)}, u32[]{:S(2)}) copy-start(bf16[1,2,3,256,256]{4,3,2,1,0:T(8,128)(2,1)} %param.5) | copy-start | bytes 2359300
  24.3 39.6 %copy-start.2 = (bf16[1,2,3,32,256]{4,3,2,1,0:T(8,128)(2,1)S(1)}, bf16[1,2,3,32,256]{4,3,2,1,0:T(8,128)(2,1)}, u32[]{:S(2)}) copy-start(bf16[1,2,3,32,256]{4,3,2,1,0:T(8,128)(2,1)} %param.4) | copy-start | bytes 294916
  24.3 19.1 %collective-permute-start.4 = (bf16[1,3,32,256]{3,2,0,1:T(8,128)(2,1)S(1)}, bf16[1,3,32,256]{3,2,0,1:T(8,128)(2,1)S(1)}, u32[]{:S(2)}, u32[]{:S(2)}) collective-permute-start(bf16[1,3,32,256]{3,2,0,1:T(8,128)(2,1)S(1)} %get-tuple-element.16), channel_id=1, source_target_pairs={{0,8},{8,16},{16,24},{24,32},{32,40},{40,48},{48,56},{1,9},{9,17},... | collective-permute-start | bytes 147464 | tf_op jit(solution)/shard_map/ppermute | solution.py:13
  26.4 17.0 %collective-permute-start.5 = (bf16[1,3,32,256]{3,2,0,1:T(8,128)(2,1)S(1)}, bf16[1,3,32,256]{3,2,0,1:T(8,128)(2,1)S(1)}, u32[]{:S(2)}, u32[]{:S(2)}) collective-permute-start(bf16[1,3,32,256]{3,2,0,1:T(8,128)(2,1)S(1)} %get-tuple-element.17), channel_id=1, source_target_pairs={{8,0},{16,8},{24,16},{32,24},{40,32},{48,40},{56,48},{9,1},{17,9},... | collective-permute-start | bytes 147464 | tf_op jit(solution)/shard_map/ppermute | solution.py:13
  32.2 5.9 %collective-permute-start.6 = (bf16[2,1,32,256]{3,2,0,1:T(8,128)(2,1)S(1)}, bf16[2,1,32,256]{3,2,0,1:T(8,128)(2,1)S(1)}, u32[]{:S(2)}, u32[]{:S(2)}) collective-permute-start(bf16[2,1,32,256]{3,2,0,1:T(8,128)(2,1)S(1)} %get-tuple-element.13), channel_id=1, source_target_pairs={{0,1},{1,2},{2,3},{3,4},{4,5},{5,6},{6,7},{8,9},{9,10},{10,11},{11... | collective-permute-start | bytes 98312 | tf_op jit(solution)/shard_map/ppermute | solution.py:13
  36.1 7.3 %collective-permute-start.7 = (bf16[2,1,32,256]{3,2,1,0:T(8,128)(2,1)S(1)}, bf16[2,1,32,256]{3,2,1,0:T(8,128)(2,1)S(1)}, u32[]{:S(2)}, u32[]{:S(2)}) collective-permute-start(bf16[2,1,32,256]{3,2,1,0:T(8,128)(2,1)S(1)} %get-tuple-element.12), channel_id=1, source_target_pairs={{1,0},{2,1},{3,2},{4,3},{5,4},{6,5},{7,6},{9,8},{10,9},{11,10},{12... | collective-permute-start | bytes 98312 | tf_op jit(solution)/shard_map/ppermute | solution.py:13
  45.3 18.6 %collective-permute-start.8 = (bf16[1,3,32,256]{3,2,0,1:T(8,128)(2,1)S(1)}, bf16[1,3,32,256]{3,2,0,1:T(8,128)(2,1)S(1)}, u32[]{:S(2)}, u32[]{:S(2)}) collective-permute-start(bf16[1,3,32,256]{3,2,0,1:T(8,128)(2,1)S(1)} %get-tuple-element.8), channel_id=1, source_target_pairs={{0,8},{8,16},{16,24},{24,32},{32,40},{40,48},{48,56},{1,9},{9,17},... | collective-permute-start | bytes 147464 | tf_op jit(solution)/shard_map/ppermute | solution.py:13
  47.2 16.7 %collective-permute-start.9 = (bf16[1,3,32,256]{3,2,0,1:T(8,128)(2,1)S(1)}, bf16[1,3,32,256]{3,2,0,1:T(8,128)(2,1)S(1)}, u32[]{:S(2)}, u32[]{:S(2)}) collective-permute-start(bf16[1,3,32,256]{3,2,0,1:T(8,128)(2,1)S(1)} %get-tuple-element.9), channel_id=1, source_target_pairs={{8,0},{16,8},{24,16},{32,24},{40,32},{48,40},{56,48},{9,1},{17,9},... | collective-permute-start | bytes 147464 | tf_op jit(solution)/shard_map/ppermute | solution.py:13
  53.0 7.1 %collective-permute-start.10 = (bf16[2,1,32,256]{3,2,0,1:T(8,128)(2,1)S(1)}, bf16[2,1,32,256]{3,2,0,1:T(8,128)(2,1)S(1)}, u32[]{:S(2)}, u32[]{:S(2)}) collective-permute-start(bf16[2,1,32,256]{3,2,0,1:T(8,128)(2,1)S(1)} %get-tuple-element.5), channel_id=1, source_target_pairs={{0,1},{1,2},{2,3},{3,4},{4,5},{5,6},{6,7},{8,9},{9,10},{10,11},{11... | collective-permute-start | bytes 98312 | tf_op jit(solution)/shard_map/ppermute | solution.py:13
  58.1 5.8 %collective-permute-start.11 = (bf16[2,1,32,256]{3,2,1,0:T(8,128)(2,1)S(1)}, bf16[2,1,32,256]{3,2,1,0:T(8,128)(2,1)S(1)}, u32[]{:S(2)}, u32[]{:S(2)}) collective-permute-start(bf16[2,1,32,256]{3,2,1,0:T(8,128)(2,1)S(1)} %get-tuple-element.4), channel_id=1, source_target_pairs={{1,0},{2,1},{3,2},{4,3},{5,4},{6,5},{7,6},{9,8},{10,9},{11,10},{12... | collective-permute-start | bytes 98312 | tf_op jit(solution)/shard_map/ppermute | solution.py:13
where the time goes:
time: 103 us
  starting transfers between devices  41.9 us (41%)
  blocking collectives  34.2 us (33%)
  waiting for transfers between devices  10.4 us (10%)
  matrix products  6.95 us (7%)
  local copies, waits for them, and re-layouts  6.77 us (7%)
  other arithmetic  1.53 us (1%)
    ppermute x12, starting transfers between devices, shifted(): return lax.ppermute(block, axis, route)  41.9 us
    psum x1, blocking collectives, shards(): summed = lax.psum(terms.astype(jnp.bfloat16), 'bias').astype(jnp.float32)  34.2 us
    ppermute x12, waiting for transfers between devices, shifted(): return lax.ppermute(block, axis, route)  10.4 us
    dot_general x3, matrix products, shards(): jnp.einsum('xyru,xyuv->xyrv', update, inverse_b, preferred_element_type=j...  3.69 us
    dot_general x3, matrix products, shards(): jnp.einsum('xyru,xyduv->xydrv', adjoint, coupling_b, preferred_element_ty...  3.26 us
  transfers between devices with their start and end apart: 12, of which 3 were waited for; matrix products, arithmetic and copies ran while one was open for 2% of the time, Pallas kernels for 0%

commit v1 on v0

--- a/solution.py
+++ b/solution.py
@@ -50,7 +50,7 @@
     shaped = adjoint.astype(jnp.float32).reshape(blocks_x, blocks_y, sides, VARS, width)
     weights = sensitivity[0].reshape(blocks_x, blocks_y, 1, VARS, width)
     terms = jnp.sum(shaped * weights, axis=3).reshape(blocks_x, blocks_y, sides * width)
-    summed = lax.psum(terms.astype(jnp.bfloat16), "bias").astype(jnp.float32)
+    summed = jnp.sum(lax.all_gather(terms.astype(jnp.bfloat16), "bias"), axis=0).astype(jnp.float32)
     share = summed.shape[2] // lax.axis_size("bias")
     doping_grad = lax.dynamic_slice_in_dim(summed, lax.axis_index("bias") * share, share, 2)
     return (adjoint[None], doping_grad)

time: 103 us -> 97.9 us (0.950)
  blocking collectives: 34.2 us -> 28.6 us
    psum x1 -> x0, blocking collectives: 34.2 us -> none  [shards(): summed = lax.psum(terms.astype(jnp.bfloat16), 'bias').astype(jnp.float32)]
    all_gather x0 -> x1, blocking collectives: none -> 28.6 us  [shards(): lax.all_gather(terms.astype(jnp.bfloat16), 'bias')]
where the time goes in v1:
time: 97.9 us; the launch traced here: 97.3 us
  starting transfers between devices  41.9 us (43%)
  blocking collectives  28.6 us (29%)
  waiting for transfers between devices  10.4 us (11%)
  matrix products  6.95 us (7%)
  local copies, waits for them, and re-layouts  6.77 us (7%)
  other arithmetic  1.72 us (2%)
    ppermute x12, starting transfers between devices, shifted(): return lax.ppermute(block, axis, route)  41.9 us
    all_gather x1, blocking collectives, shards(): lax.all_gather(terms.astype(jnp.bfloat16), 'bias')  28.6 us
    ppermute x12, waiting for transfers between devices, shifted(): return lax.ppermute(block, axis, route)  10.4 us
    dot_general x3, matrix products, shards(): jnp.einsum('xyru,xyuv->xyrv', update, inverse_b, preferred_element_type=j...  3.69 us
    dot_general x3, matrix products, shards(): jnp.einsum('xyru,xyduv->xydrv', adjoint, coupling_b, preferred_element_ty...  3.26 us
  transfers between devices with their start and end apart: 12, of which 3 were waited for; matrix products, arithmetic and copies ran while one was open for 2% of the time, Pallas kernels for 0%

profile of v1, /device:TPU:272, one launch (start us, length us, event | category | flops | bytes accessed | tf_op | source)
XLA Modules:
  0.0 97.3 jit_solution(7004550485119155490)
XLA Ops:
  0.6 1.9 %copy-done = bf16[1,2,3,4,256,256]{5,4,3,2,1,0:T(8,128)(2,1)S(1)} copy-done((bf16[1,2,3,4,256,256]{5,4,3,2,1,0:T(8,128)(2,1)S(1)}, bf16[1,2,3,4,256,256]{5,4,3,2,1,0:T(8,128)(2,1)}, u32[]{:S(2)}) %copy-start) | copy-done | bytes 3145752
  2.5 2.0 %fusion.10 = bf16[2,3,4,32,256]{4,3,2,1,0:T(8,128)(2,1)S(1)} fusion(bf16[1,2,3,256,256]{4,3,2,1,0:T(8,128)(2,1)} %param.5, bf16[1,2,3,32,256]{4,3,2,1,0:T(8,128)(2,1)} %param.4, bf16[1,2,3,4,256,256]{5,4,3,2,1,0:T(8,128)(2,1)S(1)} %copy-done), kind=kOutput, calls=%fused_computation.7 | convolution fusion | flops 126074880 | bytes 4423680 | tf_op jit(solution)/shard_map/xyru,xyduv->xydrv/dot_general | solution.py:25
  5.2 1.9 %collective-permute-start = (bf16[1,3,32,256]{3,2,1,0:T(8,128)(2,1)}, bf16[1,3,32,256]{3,2,1,0:T(8,128)(2,1)}, u32[]{:S(2)}, u32[]{:S(2)}) collective-permute-start(bf16[1,3,32,256]{3,2,1,0:T(8,128)(2,1)} %get-tuple-element.24), channel_id=1, source_target_pairs={{0,8},{8,16},{16,24},{24,32},{32,40},{40,48},{48,56},{1,9},{9,17},... | collective-permute-start | bytes 147464 | tf_op jit(solution)/shard_map/ppermute | solution.py:13
  7.1 5.8 %collective-permute-start.1 = (bf16[1,3,32,256]{3,2,1,0:T(8,128)(2,1)}, bf16[1,3,32,256]{3,2,1,0:T(8,128)(2,1)}, u32[]{:S(2)}, u32[]{:S(2)}) collective-permute-start(bf16[1,3,32,256]{3,2,1,0:T(8,128)(2,1)} %get-tuple-element.25), channel_id=1, source_target_pairs={{8,0},{16,8},{24,16},{32,24},{40,32},{48,40},{56,48},{9,1},{17,9},... | collective-permute-start | bytes 147464 | tf_op jit(solution)/shard_map/ppermute | solution.py:13
  13.5 2.3 %collective-permute-start.3 = (bf16[2,1,32,256]{3,2,0,1:T(8,128)(2,1)}, bf16[2,1,32,256]{3,2,0,1:T(8,128)(2,1)}, u32[]{:S(2)}, u32[]{:S(2)}) collective-permute-start(bf16[2,1,32,256]{3,2,0,1:T(8,128)(2,1)} %get-tuple-element.20), channel_id=1, source_target_pairs={{1,0},{2,1},{3,2},{4,3},{5,4},{6,5},{7,6},{9,8},{10,9},{11,10},{12... | collective-permute-start | bytes 98312 | tf_op jit(solution)/shard_map/ppermute | solution.py:13
  15.9 3.5 %collective-permute-start.2 = (bf16[2,1,32,256]{3,2,1,0:T(8,128)(2,1)}, bf16[2,1,32,256]{3,2,1,0:T(8,128)(2,1)}, u32[]{:S(2)}, u32[]{:S(2)}) collective-permute-start(bf16[2,1,32,256]{3,2,1,0:T(8,128)(2,1)} %get-tuple-element.21), channel_id=1, source_target_pairs={{0,1},{1,2},{2,3},{3,4},{4,5},{5,6},{6,7},{8,9},{9,10},{10,11},{11... | collective-permute-start | bytes 98312 | tf_op jit(solution)/shard_map/ppermute | solution.py:13
  20.8 1.2 %collective-permute-done.2 = bf16[2,1,32,256]{3,2,1,0:T(8,128)(2,1)} collective-permute-done((bf16[2,1,32,256]{3,2,1,0:T(8,128)(2,1)}, bf16[2,1,32,256]{3,2,1,0:T(8,128)(2,1)}, u32[]{:S(2)}, u32[]{:S(2)}) %collective-permute-start.2) | collective-permute-done | bytes 32800 | tf_op jit(solution)/shard_map/ppermute | solution.py:13
  22.0 1.6 %fusion.18 = bf16[2,3,32,256,1]{3,2,1,0,4:T(8,128)(2,1)S(1)} fusion(bf16[1,2,3,256,256]{4,3,2,1,0:T(8,128)(2,1)} %param.5, bf16[1,3,32,256]{3,2,1,0:T(8,128)(2,1)} %get-tuple-element.23, bf16[1,3,32,256]{3,2,1,0:T(8,128)(2,1)} %collective-permute-done, bf16[1,3,32,256]{3,2,1,0:T(8,128)(2,1)} %collective-permute-done.1, ...), kind=kOutput, calls=%fused_computation.15 | convolution fusion | flops 25903104 | bytes 1376256 | tf_op jit(solution)/shard_map/xyru,xyuv->xyrv/dot_general | solution.py:43
  24.3 2.1 %collective-permute-start.4 = (bf16[1,3,32,256]{3,2,0,1:T(8,128)(2,1)S(1)}, bf16[1,3,32,256]{3,2,0,1:T(8,128)(2,1)S(1)}, u32[]{:S(2)}, u32[]{:S(2)}) collective-permute-start(bf16[1,3,32,256]{3,2,0,1:T(8,128)(2,1)S(1)} %get-tuple-element.16), channel_id=1, source_target_pairs={{0,8},{8,16},{16,24},{24,32},{32,40},{40,48},{48,56},{1,9},{9,17},... | collective-permute-start | bytes 147464 | tf_op jit(solution)/shard_map/ppermute | solution.py:13
  26.4 5.8 %collective-permute-start.5 = (bf16[1,3,32,256]{3,2,0,1:T(8,128)(2,1)S(1)}, bf16[1,3,32,256]{3,2,0,1:T(8,128)(2,1)S(1)}, u32[]{:S(2)}, u32[]{:S(2)}) collective-permute-start(bf16[1,3,32,256]{3,2,0,1:T(8,128)(2,1)S(1)} %get-tuple-element.17), channel_id=1, source_target_pairs={{8,0},{16,8},{24,16},{32,24},{40,32},{48,40},{56,48},{9,1},{17,9},... | collective-permute-start | bytes 147464 | tf_op jit(solution)/shard_map/ppermute | solution.py:13
  32.2 4.0 %collective-permute-start.6 = (bf16[2,1,32,256]{3,2,0,1:T(8,128)(2,1)S(1)}, bf16[2,1,32,256]{3,2,0,1:T(8,128)(2,1)S(1)}, u32[]{:S(2)}, u32[]{:S(2)}) collective-permute-start(bf16[2,1,32,256]{3,2,0,1:T(8,128)(2,1)S(1)} %get-tuple-element.13), channel_id=1, source_target_pairs={{0,1},{1,2},{2,3},{3,4},{4,5},{5,6},{6,7},{8,9},{9,10},{10,11},{11... | collective-permute-start | bytes 98312 | tf_op jit(solution)/shard_map/ppermute | solution.py:13
  36.1 1.9 %collective-permute-start.7 = (bf16[2,1,32,256]{3,2,1,0:T(8,128)(2,1)S(1)}, bf16[2,1,32,256]{3,2,1,0:T(8,128)(2,1)S(1)}, u32[]{:S(2)}, u32[]{:S(2)}) collective-permute-start(bf16[2,1,32,256]{3,2,1,0:T(8,128)(2,1)S(1)} %get-tuple-element.12), channel_id=1, source_target_pairs={{1,0},{2,1},{3,2},{4,3},{5,4},{6,5},{7,6},{9,8},{10,9},{11,10},{12... | collective-permute-start | bytes 98312 | tf_op jit(solution)/shard_map/ppermute | solution.py:13
  38.1 5.4 %collective-permute-done.7 = bf16[2,1,32,256]{3,2,1,0:T(8,128)(2,1)S(1)} collective-permute-done((bf16[2,1,32,256]{3,2,1,0:T(8,128)(2,1)S(1)}, bf16[2,1,32,256]{3,2,1,0:T(8,128)(2,1)S(1)}, u32[]{:S(2)}, u32[]{:S(2)}) %collective-permute-start.7) | collective-permute-done | bytes 32800 | tf_op jit(solution)/shard_map/ppermute | solution.py:13
  43.5 1.1 %fusion.19 = bf16[2,3,32,256,1]{3,2,1,0,4:T(8,128)(2,1)S(1)} fusion(bf16[1,2,3,256,256]{4,3,2,1,0:T(8,128)(2,1)S(1)} %copy-done.1, bf16[2,1,32,256]{3,2,1,0:T(8,128)(2,1)S(1)} %collective-permute-done.7, bf16[1,2,3,32,256]{4,3,2,1,0:T(8,128)(2,1)} %param.4, bf16[1,3,32,256]{3,2,0,1:T(8,128)(2,1)S(1)} %get-tuple-element.15, ...), kind=kOutput, calls=%fused_computation.16 | convolution fusion | flops 26001408 | bytes 1376256 | tf_op jit(solution)/shard_map/xyru,xyuv->xyrv/dot_general | solution.py:43
  45.3 1.9 %collective-permute-start.8 = (bf16[1,3,32,256]{3,2,0,1:T(8,128)(2,1)S(1)}, bf16[1,3,32,256]{3,2,0,1:T(8,128)(2,1)S(1)}, u32[]{:S(2)}, u32[]{:S(2)}) collective-permute-start(bf16[1,3,32,256]{3,2,0,1:T(8,128)(2,1)S(1)} %get-tuple-element.8), channel_id=1, source_target_pairs={{0,8},{8,16},{16,24},{24,32},{32,40},{40,48},{48,56},{1,9},{9,17},... | collective-permute-start | bytes 147464 | tf_op jit(solution)/shard_map/ppermute | solution.py:13
  47.2 5.8 %collective-permute-start.9 = (bf16[1,3,32,256]{3,2,0,1:T(8,128)(2,1)S(1)}, bf16[1,3,32,256]{3,2,0,1:T(8,128)(2,1)S(1)}, u32[]{:S(2)}, u32[]{:S(2)}) collective-permute-start(bf16[1,3,32,256]{3,2,0,1:T(8,128)(2,1)S(1)} %get-tuple-element.9), channel_id=1, source_target_pairs={{8,0},{16,8},{24,16},{32,24},{40,32},{48,40},{56,48},{9,1},{17,9},... | collective-permute-start | bytes 147464 | tf_op jit(solution)/shard_map/ppermute | solution.py:13
  53.0 5.1 %collective-permute-start.10 = (bf16[2,1,32,256]{3,2,0,1:T(8,128)(2,1)S(1)}, bf16[2,1,32,256]{3,2,0,1:T(8,128)(2,1)S(1)}, u32[]{:S(2)}, u32[]{:S(2)}) collective-permute-start(bf16[2,1,32,256]{3,2,0,1:T(8,128)(2,1)S(1)} %get-tuple-element.5), channel_id=1, source_target_pairs={{0,1},{1,2},{2,3},{3,4},{4,5},{5,6},{6,7},{8,9},{9,10},{10,11},{11... | collective-permute-start | bytes 98312 | tf_op jit(solution)/shard_map/ppermute | solution.py:13
  58.1 1.9 %collective-permute-start.11 = (bf16[2,1,32,256]{3,2,1,0:T(8,128)(2,1)S(1)}, bf16[2,1,32,256]{3,2,1,0:T(8,128)(2,1)S(1)}, u32[]{:S(2)}, u32[]{:S(2)}) collective-permute-start(bf16[2,1,32,256]{3,2,1,0:T(8,128)(2,1)S(1)} %get-tuple-element.4), channel_id=1, source_target_pairs={{1,0},{2,1},{3,2},{4,3},{5,4},{6,5},{7,6},{9,8},{10,9},{11,10},{12... | collective-permute-start | bytes 98312 | tf_op jit(solution)/shard_map/ppermute | solution.py:13
  60.1 3.9 %collective-permute-done.11 = bf16[2,1,32,256]{3,2,1,0:T(8,128)(2,1)S(1)} collective-permute-done((bf16[2,1,32,256]{3,2,1,0:T(8,128)(2,1)S(1)}, bf16[2,1,32,256]{3,2,1,0:T(8,128)(2,1)S(1)}, u32[]{:S(2)}, u32[]{:S(2)}) %collective-permute-start.11) | collective-permute-done | bytes 32800 | tf_op jit(solution)/shard_map/ppermute | solution.py:13
  64.0 0.9 convolution_convert_fusion.1
  64.9 1.1 %reshape.26 = f32[2,3,32,4,64]{4,3,2,1,0:T(4,128)S(1)} reshape(bf16[2,3,32,256]{3,2,1,0:T(8,128)(2,1)} %convolution_convert_fusion.1) | data formatting | bytes 294912 | tf_op jit(solution)/shard_map/reshape | solution.py:50
  66.0 0.9 multiply_reduce_fusion
  66.9 0.9 reshape.30
  67.8 28.6 %all_gather.4 = bf16[8,2,3,2048]{3,1,2,0:T(2,128)(2,1)S(1)} all-gather(bf16[1,2,3,2048]{3,1,2,0:T(2,128)(2,1)S(1)} %copy.79), channel_id=1, replica_groups=mesh['bias'=8,'gx'=8,'gy'=8] {'bias'}, dimensions={0}, use_global_device_ids=true | all-gather | bytes 221184 | tf_op jit(solution)/shard_map/all_gather | solution.py:53
  (29 shorter events, 5.0 us)
Async XLA Ops:
  0.6 1.9 %copy-start = (bf16[1,2,3,4,256,256]{5,4,3,2,1,0:T(8,128)(2,1)S(1)}, bf16[1,2,3,4,256,256]{5,4,3,2,1,0:T(8,128)(2,1)}, u32[]{:S(2)}) copy-start(bf16[1,2,3,4,256,256]{5,4,3,2,1,0:T(8,128)(2,1)} %param.6) | copy-start | bytes 9437188
  5.2 16.8 %collective-permute-start = (bf16[1,3,32,256]{3,2,1,0:T(8,128)(2,1)}, bf16[1,3,32,256]{3,2,1,0:T(8,128)(2,1)}, u32[]{:S(2)}, u32[]{:S(2)}) collective-permute-start(bf16[1,3,32,256]{3,2,1,0:T(8,128)(2,1)} %get-tuple-element.24), channel_id=1, source_target_pairs={{0,8},{8,16},{16,24},{24,32},{32,40},{40,48},{48,56},{1,9},{9,17},... | collective-permute-start | bytes 147464 | tf_op jit(solution)/shard_map/ppermute | solution.py:13
  7.1 14.9 %collective-permute-start.1 = (bf16[1,3,32,256]{3,2,1,0:T(8,128)(2,1)}, bf16[1,3,32,256]{3,2,1,0:T(8,128)(2,1)}, u32[]{:S(2)}, u32[]{:S(2)}) collective-permute-start(bf16[1,3,32,256]{3,2,1,0:T(8,128)(2,1)} %get-tuple-element.25), channel_id=1, source_target_pairs={{8,0},{16,8},{24,16},{32,24},{40,32},{48,40},{56,48},{9,1},{17,9},... | collective-permute-start | bytes 147464 | tf_op jit(solution)/shard_map/ppermute | solution.py:13
  13.5 7.3 %collective-permute-start.3 = (bf16[2,1,32,256]{3,2,0,1:T(8,128)(2,1)}, bf16[2,1,32,256]{3,2,0,1:T(8,128)(2,1)}, u32[]{:S(2)}, u32[]{:S(2)}) collective-permute-start(bf16[2,1,32,256]{3,2,0,1:T(8,128)(2,1)} %get-tuple-element.20), channel_id=1, source_target_pairs={{1,0},{2,1},{3,2},{4,3},{5,4},{6,5},{7,6},{9,8},{10,9},{11,10},{12... | collective-permute-start | bytes 98312 | tf_op jit(solution)/shard_map/ppermute | solution.py:13
  15.9 6.1 %collective-permute-start.2 = (bf16[2,1,32,256]{3,2,1,0:T(8,128)(2,1)}, bf16[2,1,32,256]{3,2,1,0:T(8,128)(2,1)}, u32[]{:S(2)}, u32[]{:S(2)}) collective-permute-start(bf16[2,1,32,256]{3,2,1,0:T(8,128)(2,1)} %get-tuple-element.21), channel_id=1, source_target_pairs={{0,1},{1,2},{2,3},{3,4},{4,5},{5,6},{6,7},{8,9},{9,10},{10,11},{11... | collective-permute-start | bytes 98312 | tf_op jit(solution)/shard_map/ppermute | solution.py:13
  20.8 22.7 %copy-start.1 = (bf16[1,2,3,256,256]{4,3,2,1,0:T(8,128)(2,1)S(1)}, bf16[1,2,3,256,256]{4,3,2,1,0:T(8,128)(2,1)}, u32[]{:S(2)}) copy-start(bf16[1,2,3,256,256]{4,3,2,1,0:T(8,128)(2,1)} %param.5) | copy-start | bytes 2359300
  24.3 39.6 %copy-start.2 = (bf16[1,2,3,32,256]{4,3,2,1,0:T(8,128)(2,1)S(1)}, bf16[1,2,3,32,256]{4,3,2,1,0:T(8,128)(2,1)}, u32[]{:S(2)}) copy-start(bf16[1,2,3,32,256]{4,3,2,1,0:T(8,128)(2,1)} %param.4) | copy-start | bytes 294916
  24.3 19.1 %collective-permute-start.4 = (bf16[1,3,32,256]{3,2,0,1:T(8,128)(2,1)S(1)}, bf16[1,3,32,256]{3,2,0,1:T(8,128)(2,1)S(1)}, u32[]{:S(2)}, u32[]{:S(2)}) collective-permute-start(bf16[1,3,32,256]{3,2,0,1:T(8,128)(2,1)S(1)} %get-tuple-element.16), channel_id=1, source_target_pairs={{0,8},{8,16},{16,24},{24,32},{32,40},{40,48},{48,56},{1,9},{9,17},... | collective-permute-start | bytes 147464 | tf_op jit(solution)/shard_map/ppermute | solution.py:13
  26.4 17.0 %collective-permute-start.5 = (bf16[1,3,32,256]{3,2,0,1:T(8,128)(2,1)S(1)}, bf16[1,3,32,256]{3,2,0,1:T(8,128)(2,1)S(1)}, u32[]{:S(2)}, u32[]{:S(2)}) collective-permute-start(bf16[1,3,32,256]{3,2,0,1:T(8,128)(2,1)S(1)} %get-tuple-element.17), channel_id=1, source_target_pairs={{8,0},{16,8},{24,16},{32,24},{40,32},{48,40},{56,48},{9,1},{17,9},... | collective-permute-start | bytes 147464 | tf_op jit(solution)/shard_map/ppermute | solution.py:13
  32.2 5.9 %collective-permute-start.6 = (bf16[2,1,32,256]{3,2,0,1:T(8,128)(2,1)S(1)}, bf16[2,1,32,256]{3,2,0,1:T(8,128)(2,1)S(1)}, u32[]{:S(2)}, u32[]{:S(2)}) collective-permute-start(bf16[2,1,32,256]{3,2,0,1:T(8,128)(2,1)S(1)} %get-tuple-element.13), channel_id=1, source_target_pairs={{0,1},{1,2},{2,3},{3,4},{4,5},{5,6},{6,7},{8,9},{9,10},{10,11},{11... | collective-permute-start | bytes 98312 | tf_op jit(solution)/shard_map/ppermute | solution.py:13
  36.1 7.3 %collective-permute-start.7 = (bf16[2,1,32,256]{3,2,1,0:T(8,128)(2,1)S(1)}, bf16[2,1,32,256]{3,2,1,0:T(8,128)(2,1)S(1)}, u32[]{:S(2)}, u32[]{:S(2)}) collective-permute-start(bf16[2,1,32,256]{3,2,1,0:T(8,128)(2,1)S(1)} %get-tuple-element.12), channel_id=1, source_target_pairs={{1,0},{2,1},{3,2},{4,3},{5,4},{6,5},{7,6},{9,8},{10,9},{11,10},{12... | collective-permute-start | bytes 98312 | tf_op jit(solution)/shard_map/ppermute | solution.py:13
  45.3 18.6 %collective-permute-start.8 = (bf16[1,3,32,256]{3,2,0,1:T(8,128)(2,1)S(1)}, bf16[1,3,32,256]{3,2,0,1:T(8,128)(2,1)S(1)}, u32[]{:S(2)}, u32[]{:S(2)}) collective-permute-start(bf16[1,3,32,256]{3,2,0,1:T(8,128)(2,1)S(1)} %get-tuple-element.8), channel_id=1, source_target_pairs={{0,8},{8,16},{16,24},{24,32},{32,40},{40,48},{48,56},{1,9},{9,17},... | collective-permute-start | bytes 147464 | tf_op jit(solution)/shard_map/ppermute | solution.py:13
  47.2 16.7 %collective-permute-start.9 = (bf16[1,3,32,256]{3,2,0,1:T(8,128)(2,1)S(1)}, bf16[1,3,32,256]{3,2,0,1:T(8,128)(2,1)S(1)}, u32[]{:S(2)}, u32[]{:S(2)}) collective-permute-start(bf16[1,3,32,256]{3,2,0,1:T(8,128)(2,1)S(1)} %get-tuple-element.9), channel_id=1, source_target_pairs={{8,0},{16,8},{24,16},{32,24},{40,32},{48,40},{56,48},{9,1},{17,9},... | collective-permute-start | bytes 147464 | tf_op jit(solution)/shard_map/ppermute | solution.py:13
  53.0 7.1 %collective-permute-start.10 = (bf16[2,1,32,256]{3,2,0,1:T(8,128)(2,1)S(1)}, bf16[2,1,32,256]{3,2,0,1:T(8,128)(2,1)S(1)}, u32[]{:S(2)}, u32[]{:S(2)}) collective-permute-start(bf16[2,1,32,256]{3,2,0,1:T(8,128)(2,1)S(1)} %get-tuple-element.5), channel_id=1, source_target_pairs={{0,1},{1,2},{2,3},{3,4},{4,5},{5,6},{6,7},{8,9},{9,10},{10,11},{11... | collective-permute-start | bytes 98312 | tf_op jit(solution)/shard_map/ppermute | solution.py:13
  58.1 5.8 %collective-permute-start.11 = (bf16[2,1,32,256]{3,2,1,0:T(8,128)(2,1)S(1)}, bf16[2,1,32,256]{3,2,1,0:T(8,128)(2,1)S(1)}, u32[]{:S(2)}, u32[]{:S(2)}) collective-permute-start(bf16[2,1,32,256]{3,2,1,0:T(8,128)(2,1)S(1)} %get-tuple-element.4), channel_id=1, source_target_pairs={{1,0},{2,1},{3,2},{4,3},{5,4},{6,5},{7,6},{9,8},{10,9},{11,10},{12... | collective-permute-start | bytes 98312 | tf_op jit(solution)/shard_map/ppermute | solution.py:13
